TPU v7x, 32 devices: a whole 2x2x4 slice. The times are simulated.
32 devices in a mesh: dp: 4 (over z), fsdp: 8 (over y, x, core).
Axes of the slice: x: 2, y: 2, z: 4, core: 2. Of those that a mesh axis runs over, the one named last changes fastest.
Arguments:
- tokens: bfloat16 [32, 448, 768], P(('dp', 'fsdp')), may hold values from -6 to 6
- enc_states: bfloat16 [32, 1500, 768], P(('dp', 'fsdp')), may hold values from -6 to 6
- cotangent: bfloat16 [32, 448, 768], P(('dp', 'fsdp')), may hold values from -6 to 6
- tok_len: int32 [32], P(('dp', 'fsdp')), may hold values from 224 to 448, as said below
- frame_count: int32 [32], P(('dp', 'fsdp')), may hold values from 750 to 1500, as said below
- attn_w: float32 [8, 768, 768], P(None, ('dp', 'fsdp'))
- attn_m: float32 [8, 768, 768], P(None, ('dp', 'fsdp')), may hold values from -40 to 40
- attn_v: float32 [8, 768, 768], P(None, ('dp', 'fsdp')), may hold values from 1.792 to 28.672
- mlp_w: float32 [2, 3072, 768], P(None, ('dp', 'fsdp')), may hold values from -0.21875 to 0.21875
- mlp_m: float32 [2, 3072, 768], P(None, ('dp', 'fsdp')), may hold values from -40 to 40
- mlp_v: float32 [2, 3072, 768], P(None, ('dp', 'fsdp')), may hold values from 1.792 to 28.672
- vec_w: float32 [17, 768], P(None, ('dp', 'fsdp'))
- vec_m: float32 [17, 768], P(None, ('dp', 'fsdp')), may hold values from -80 to 80
- vec_v: float32 [17, 768], P(None, ('dp', 'fsdp')), may hold values from 7.168 to 114.688
Outputs:
- out: bfloat16 [32, 448, 768], P(('dp', 'fsdp'))
- d_tokens: float32 [32, 448, 768], P(('dp', 'fsdp'))
- d_enc: float32 [32, 1500, 768], P(('dp', 'fsdp'))
- attn_w_new: float32 [8, 768, 768], P(None, ('dp', 'fsdp'))
- attn_m_new: float32 [8, 768, 768], P(None, ('dp', 'fsdp'))
- attn_v_new: float32 [8, 768, 768], P(None, ('dp', 'fsdp'))
- mlp_w_new: float32 [2, 3072, 768], P(None, ('dp', 'fsdp'))
- mlp_m_new: float32 [2, 3072, 768], P(None, ('dp', 'fsdp'))
- mlp_v_new: float32 [2, 3072, 768], P(None, ('dp', 'fsdp'))
- vec_w_new: float32 [17, 768], P(None, ('dp', 'fsdp'))
- vec_m_new: float32 [17, 768], P(None, ('dp', 'fsdp'))
- vec_v_new: float32 [17, 768], P(None, ('dp', 'fsdp'))
Inputs may be any that keep to these rules, and one draw needn't show every extreme that they name: `tok_len`: at least 224 slots of every clip are valid, and some clip has all 448. `frame_count`: at least 750 frames of every clip are valid, and some clip has all 1500.
All inputs are finite; a program needn't handle non-finite values.
Results may differ from a plain program's by a relative error of at most 0.018.
The roundings to bfloat16 on the way count: a program that leaves them out, or rounds other values in their place, can miss the bound.
Values may be sent and summed in bfloat16 or wider, within the bound.
A program may use at most 256 MiB of HBM per device.

v0:
```python
import jax
import jax.numpy as jnp
from jax import lax
from jax.sharding import PartitionSpec as P

D = 768
H = 12
HD = 64
FF = 3072
FRAMES = 1500
TOK = 448
STEP = 10


norm_epsilon = 1e-05
beta_first = 0.9
beta_second = 0.999
adam_epsilon = 1e-08
weight_decay = 0.01
rate_attention = 0.06
rate_feedforward = 0.03
rate_vector = 0.35


def matmul(left, right):
    return jnp.dot(left, right, preferred_element_type=jnp.float32)


def inner_rows(left, right):
    return lax.dot_general(
        left, right, (((0,), (0,)), ((), ())), preferred_element_type=jnp.float32
    )


def outer_last(left, right):
    return lax.dot_general(
        left, right, (((1,), (1,)), ((), ())), preferred_element_type=jnp.float32
    )


def norm_apply(value, gain, shift):
    center = value - jnp.mean(value, -1, keepdims=True)
    spread = jnp.mean(center * center, -1, keepdims=True)
    return center * lax.rsqrt(spread + norm_epsilon) * gain + shift


def gelu_exact(value):
    return jax.nn.gelu(value, approximate=False)


def head_group():
    return 4


def grouped(value):
    width = head_group()
    return (
        value.reshape(value.shape[0], H, HD)
        .transpose(1, 0, 2)
        .reshape(H // width, width, value.shape[0], HD)
    )


def ungrouped(value):
    return value.reshape(H, value.shape[2], HD).transpose(1, 0, 2).reshape(value.shape[2], H * HD)


def attend_forward(query, keys, values, mask):

    def one_group(parts):
        q_group, k_group, v_group = parts
        scores = jnp.einsum("gtd,gsd->gts", q_group, k_group, preferred_element_type=jnp.float32)
        scores = jnp.where(mask[None], scores, -1e30)
        peak = jnp.max(scores, -1, keepdims=True)
        expo = jnp.exp(scores - peak)
        total = jnp.sum(expo, -1, keepdims=True)
        probs = (expo / total).astype(jnp.bfloat16)
        mixed = jnp.einsum("gts,gsd->gtd", probs, v_group, preferred_element_type=jnp.float32)
        return (mixed.astype(jnp.bfloat16), (peak + jnp.log(total))[..., 0])

    heads, summed = lax.map(one_group, (grouped(query), grouped(keys), grouped(values)))
    return (ungrouped(heads), summed)


def attend_backward(query, keys, values, summed, grad_out, mask):

    def one_group(parts):
        q_group, k_group, v_group, s_group, g_group = parts
        scores = jnp.einsum("gtd,gsd->gts", q_group, k_group, preferred_element_type=jnp.float32)
        probs = jnp.where(mask[None], jnp.exp(scores - s_group[..., None]), 0.0)
        grad_values = jnp.einsum(
            "gts,gtd->gsd", probs.astype(jnp.bfloat16), g_group, preferred_element_type=jnp.float32
        )
        grad_probs = jnp.einsum(
            "gtd,gsd->gts", g_group, v_group, preferred_element_type=jnp.float32
        )
        grad_scores = (
            probs * (grad_probs - jnp.sum(probs * grad_probs, -1, keepdims=True))
        ).astype(jnp.bfloat16)
        grad_query = jnp.einsum(
            "gts,gsd->gtd", grad_scores, k_group, preferred_element_type=jnp.float32
        ).astype(jnp.bfloat16)
        grad_keys = jnp.einsum(
            "gts,gtd->gsd", grad_scores, q_group, preferred_element_type=jnp.float32
        ).astype(jnp.bfloat16)
        return (grad_query, grad_keys, grad_values.astype(jnp.bfloat16))

    parts = (grouped(query), grouped(keys), grouped(values), summed, grouped(grad_out))
    grad_query, grad_keys, grad_values = lax.map(one_group, parts)
    return (ungrouped(grad_query), ungrouped(grad_keys), ungrouped(grad_values))


def make_masks(length, frames):
    place = jnp.arange(TOK)
    causal = (place[None, :] <= place[:, None]) & (place[None, :] < length)
    seen = jnp.broadcast_to(jnp.arange(FRAMES)[None, :] < frames, (TOK, FRAMES))
    return (place, causal, seen)


def clip_forward(weights, x_in, enc, length, frames):
    wa, wm, wv = weights
    vec = wv.astype(jnp.float32)
    scale = HD ** (-0.5)
    place, causal, seen = make_masks(length, frames)
    x = x_in.astype(jnp.float32)
    first = norm_apply(x, vec[0], vec[1]).astype(jnp.bfloat16)
    query = ((matmul(first, wa[0]) + vec[6]) * scale).astype(jnp.bfloat16)
    keys = matmul(first, wa[1]).astype(jnp.bfloat16)
    values = (matmul(first, wa[2]) + vec[7]).astype(jnp.bfloat16)
    mixed, summed_self = attend_forward(query, keys, values, causal)
    second_in = x + matmul(mixed, wa[3]) + vec[8]
    second = norm_apply(second_in, vec[2], vec[3]).astype(jnp.bfloat16)
    cross_query = ((matmul(second, wa[4]) + vec[9]) * scale).astype(jnp.bfloat16)
    cross_keys = matmul(enc, wa[5]).astype(jnp.bfloat16)
    cross_values = (matmul(enc, wa[6]) + vec[10]).astype(jnp.bfloat16)
    heard, summed_cross = attend_forward(cross_query, cross_keys, cross_values, seen)
    third_in = second_in + matmul(heard, wa[7]) + vec[11]
    third = norm_apply(third_in, vec[4], vec[5]).astype(jnp.bfloat16)
    hidden_pre = outer_last(third, wm[0]) + vec[13:].reshape(FF)
    hidden = gelu_exact(hidden_pre).astype(jnp.bfloat16)
    result = third_in + matmul(hidden, wm[1]) + vec[12]
    saved = (
        first,
        query,
        keys,
        values,
        mixed,
        summed_self,
        second_in,
        second,
        cross_query,
        cross_keys,
        cross_values,
        heard,
        summed_cross,
        third_in,
        third,
        hidden_pre,
        hidden,
    )
    return (result.astype(jnp.bfloat16), saved)


def clip_backward(weights, x_in, enc, length, frames, cot, saved):
    wa, wm, wv = weights
    vec = wv.astype(jnp.float32)
    scale = HD ** (-0.5)
    (
        first,
        query,
        keys,
        values,
        mixed,
        summed_self,
        second_in,
        second,
        cross_query,
        cross_keys,
        cross_values,
        heard,
        summed_cross,
        third_in,
        third,
        hidden_pre,
        hidden,
    ) = saved
    place, causal, seen = make_masks(length, frames)
    grad_y = cot.astype(jnp.float32) * (place < length).astype(jnp.float32)[:, None]
    out_three = grad_y.astype(jnp.bfloat16)
    g_down = inner_rows(hidden, out_three)
    g_b_down = jnp.sum(out_three.astype(jnp.float32), 0)
    grad_hidden = outer_last(out_three, wm[1])
    _, gelu_pull = jax.vjp(gelu_exact, hidden_pre)
    grad_pre = gelu_pull(grad_hidden)[0].astype(jnp.bfloat16)
    g_up = inner_rows(grad_pre, third)
    g_b_up = jnp.sum(grad_pre.astype(jnp.float32), 0)
    grad_third = matmul(grad_pre, wm[0])
    _, norm_pull = jax.vjp(norm_apply, third_in, vec[4], vec[5])
    part_three, g_gain_three, g_shift_three = norm_pull(grad_third)
    grad_third_in = grad_y + part_three
    out_two = grad_third_in.astype(jnp.bfloat16)
    g_cross_out = inner_rows(heard, out_two)
    g_b_cross_out = jnp.sum(out_two.astype(jnp.float32), 0)
    grad_heard = outer_last(out_two, wa[7]).astype(jnp.bfloat16)
    grad_cq, grad_ck, grad_cv = attend_backward(
        cross_query, cross_keys, cross_values, summed_cross, grad_heard, seen
    )
    grad_cq = grad_cq * scale
    g_cross_query = inner_rows(second, grad_cq)
    g_b_cross_query = jnp.sum(grad_cq.astype(jnp.float32), 0)
    g_cross_keys = inner_rows(enc, grad_ck)
    g_cross_values = inner_rows(enc, grad_cv)
    g_b_cross_values = jnp.sum(grad_cv.astype(jnp.float32), 0)
    grad_enc = outer_last(grad_ck, wa[5]) + outer_last(grad_cv, wa[6])
    grad_second = outer_last(grad_cq, wa[4])
    _, norm_pull = jax.vjp(norm_apply, second_in, vec[2], vec[3])
    part_two, g_gain_two, g_shift_two = norm_pull(grad_second)
    grad_second_in = grad_third_in + part_two
    out_one = grad_second_in.astype(jnp.bfloat16)
    g_self_out = inner_rows(mixed, out_one)
    g_b_self_out = jnp.sum(out_one.astype(jnp.float32), 0)
    grad_mixed = outer_last(out_one, wa[3]).astype(jnp.bfloat16)
    grad_q, grad_k, grad_v = attend_backward(query, keys, values, summed_self, grad_mixed, causal)
    grad_q = grad_q * scale
    g_self_query = inner_rows(first, grad_q)
    g_self_keys = inner_rows(first, grad_k)
    g_self_values = inner_rows(first, grad_v)
    g_b_self_query = jnp.sum(grad_q.astype(jnp.float32), 0)
    g_b_self_values = jnp.sum(grad_v.astype(jnp.float32), 0)
    grad_first = outer_last(grad_q, wa[0]) + outer_last(grad_k, wa[1]) + outer_last(grad_v, wa[2])
    _, norm_pull = jax.vjp(norm_apply, x_in.astype(jnp.float32), vec[0], vec[1])
    part_one, g_gain_one, g_shift_one = norm_pull(grad_first)
    grad_x = grad_second_in + part_one
    g_attn = jnp.stack(
        [
            g_self_query,
            g_self_keys,
            g_self_values,
            g_self_out,
            g_cross_query,
            g_cross_keys,
            g_cross_values,
            g_cross_out,
        ]
    )
    g_mlp = jnp.stack([g_up, g_down])
    g_vec = jnp.concatenate(
        [
            jnp.stack(
                [
                    g_gain_one,
                    g_shift_one,
                    g_gain_two,
                    g_shift_two,
                    g_gain_three,
                    g_shift_three,
                    g_b_self_query,
                    g_b_self_values,
                    g_b_self_out,
                    g_b_cross_query,
                    g_b_cross_values,
                    g_b_cross_out,
                    g_b_down,
                ]
            ),
            g_b_up.reshape(FF // D, D),
        ],
        0,
    )
    return ((g_attn, g_mlp, g_vec), grad_x, grad_enc)


def adam_update(weight, first, second, grad, rate):
    first_new = beta_first * first + (1.0 - beta_first) * grad
    second_new = beta_second * second + (1.0 - beta_second) * grad * grad
    ratio = (
        first_new
        / (1.0 - beta_first**STEP)
        / (jnp.sqrt(second_new / (1.0 - beta_second**STEP)) + adam_epsilon)
    )
    return (weight - rate * (ratio + weight_decay * weight), first_new, second_new)


def body(
    tokens,
    enc_states,
    cotangent,
    tok_len,
    frame_count,
    attn_w,
    attn_m,
    attn_v,
    mlp_w,
    mlp_m,
    mlp_v,
    vec_w,
    vec_m,
    vec_v,
):
    shards = (attn_w.astype(jnp.bfloat16), mlp_w.astype(jnp.bfloat16), vec_w.astype(jnp.bfloat16))
    weights = (
        lax.all_gather(shards[0], ("dp", "fsdp"), axis=1, tiled=True),
        lax.all_gather(shards[1], ("dp", "fsdp"), axis=1, tiled=True),
        lax.all_gather(shards[2], ("dp", "fsdp"), axis=1, tiled=True),
    )

    def forward_one(items):
        x_in, enc, length, frames = items
        return clip_forward(weights, x_in, enc, length, frames)

    result, saved = lax.map(forward_one, (tokens, enc_states, tok_len, frame_count))
    back_weights = (
        lax.all_gather(shards[0], ("dp", "fsdp"), axis=1, tiled=True),
        lax.all_gather(shards[1], ("dp", "fsdp"), axis=1, tiled=True),
        lax.all_gather(shards[2], ("dp", "fsdp"), axis=1, tiled=True),
    )

    def backward_one(carry, items):
        x_in, enc, length, frames, cot, kept = items
        grads, grad_x, grad_enc = clip_backward(back_weights, x_in, enc, length, frames, cot, kept)
        return (jax.tree.map(jnp.add, carry, grads), (grad_x, grad_enc))

    zeros = (
        jnp.zeros(weights[0].shape, jnp.float32),
        jnp.zeros(weights[1].shape, jnp.float32),
        jnp.zeros(weights[2].shape, jnp.float32),
    )
    totals, (d_tokens, d_enc) = lax.scan(
        backward_one, zeros, (tokens, enc_states, tok_len, frame_count, cotangent, saved)
    )
    grad_attn, grad_mlp, grad_vec = (
        lax.psum_scatter(totals[0], ("dp", "fsdp"), scatter_dimension=1, tiled=True),
        lax.psum_scatter(totals[1], ("dp", "fsdp"), scatter_dimension=1, tiled=True),
        lax.psum_scatter(totals[2], ("dp", "fsdp"), scatter_dimension=1, tiled=True),
    )
    attn_new = adam_update(attn_w, attn_m, attn_v, grad_attn, rate_attention)
    mlp_new = adam_update(mlp_w, mlp_m, mlp_v, grad_mlp, rate_feedforward)
    vec_new = adam_update(vec_w, vec_m, vec_v, grad_vec, rate_vector)
    return (
        result,
        d_tokens,
        d_enc,
        attn_new[0],
        attn_new[1],
        attn_new[2],
        mlp_new[0],
        mlp_new[1],
        mlp_new[2],
        vec_new[0],
        vec_new[1],
        vec_new[2],
    )


def solution(mesh):
    return jax.shard_map(
        body,
        mesh=mesh,
        in_specs=(
            P(("dp", "fsdp"), None, None),
            P(("dp", "fsdp"), None, None),
            P(("dp", "fsdp"), None, None),
            P(("dp", "fsdp")),
            P(("dp", "fsdp")),
            P(None, ("dp", "fsdp"), None),
            P(None, ("dp", "fsdp"), None),
            P(None, ("dp", "fsdp"), None),
            P(None, ("dp", "fsdp"), None),
            P(None, ("dp", "fsdp"), None),
            P(None, ("dp", "fsdp"), None),
            P(None, ("dp", "fsdp")),
            P(None, ("dp", "fsdp")),
            P(None, ("dp", "fsdp")),
        ),
        out_specs=(
            P(("dp", "fsdp"), None, None),
            P(("dp", "fsdp"), None, None),
            P(("dp", "fsdp"), None, None),
            P(None, ("dp", "fsdp"), None),
            P(None, ("dp", "fsdp"), None),
            P(None, ("dp", "fsdp"), None),
            P(None, ("dp", "fsdp"), None),
            P(None, ("dp", "fsdp"), None),
            P(None, ("dp", "fsdp"), None),
            P(None, ("dp", "fsdp")),
            P(None, ("dp", "fsdp")),
            P(None, ("dp", "fsdp")),
        ),
        check_vma=False,
    )
```

profile of v0, /device:TPU:0, one launch (start us, length us, event | category | flops | bytes accessed | tf_op | source)
XLA Modules:
  0.0 788.1 jit_solution(16960731587927173352)
XLA Ops:
  11.3 44.3 %all_gather.12 = bf16[17,768]{0,1:T(8,128)(2,1)S(1)} all-gather(bf16[17,24]{0,1:T(8,128)(2,1)S(1)} %copy.76), channel_id=1, replica_groups=mesh['dp'=4,'fsdp'=8] {'dp','fsdp'}, dimensions={1}, use_global_device_ids=true | all-gather | bytes 26928 | tf_op jit(solution)/shard_map/all_gather | solution.py:304
  63.4 33.3 %all-gather.3.cloned.1.call-done = bf16[8,768,768]{2,1,0:T(8,128)(2,1)} async-done(((bf16[8,24,768]{2,1,0:T(8,128)(2,1)}), bf16[8,768,768]{2,1,0:T(8,128)(2,1)}) %all-gather.3.cloned.1.call-update) | async-done | bytes 9437200 | tf_op jit(solution)/shard_map/all_gather | solution.py:302
  112.7 16.4 %while.103 = (s32[]{:T(128)}, bf16[3,4,448,64]{2,3,1,0:T(8,128)(2,1)}, f32[3,4,448]{2,1,0:T(4,128)S(1)}, bf16[3,4,448,64]{2,3,1,0:T(8,128)(2,1)S(1)}, bf16[3,4,4...) while((s32[]{:T(128)}, ...), condition=%wide.region_5.6_spmd.clone, body=%wide.region_2.0_spmd.clone.sunk | while | flops 213260544 | bytes 11576865 | solution.py:81
  137.5 4.6 convolution_convert_fusion.4
  142.2 4.3 copy.81
  146.5 4.6 add_convert_fusion.1
  151.1 4.3 copy.82
  156.4 28.2 %while.104 = (s32[]{:T(128)}, bf16[3,4,448,64]{2,3,1,0:T(8,128)(2,1)}, f32[3,4,448]{2,1,0:T(4,128)S(1)}, bf16[3,4,448,64]{2,3,1,0:T(8,128)(2,1)S(1)}, bf16[3,4,1...) while((s32[]{:T(128)}, ...), condition=%wide.region_11.12_spmd.clone, body=%wide.region_8.11_spmd.clone.sunk | while | flops 712432896 | bytes 34420760 | solution.py:81
  161.6 4.4 fusion.266
  170.9 4.4 fusion.266
  180.2 4.4 fusion.266
  189.0 18.0 %multiply_convert_fusion.2 = (bf16[448,3072]{1,0:T(8,128)(2,1)}, f32[448,3072]{1,0:T(8,128)}, f32[448,3072]{1,0:T(8,128)}) fusion(f32[3072]{0:T(1024)S(1)} %copy-done.65, bf16[2,3072,768]{2,1,0:T(8,128)(2,1)} %all-gather.5.cloned.1.call-done, f32[448,768]{1,0:T(8,128)} %copy-done.5, f32[768]{0:T(1024)S(1)} %copy-done.75, f32[768]{0:T(1024)S(1)} %copy-done.59, ...), kind=kOutput, calls=%fused_computation.133 | convolution fusion | flops 2206482432 | bytes 19879424 | tf_op jit(solution)/shard_map/while/body/eval_jaxpr/dot_general | solution.py:36
  207.0 7.7 convert_reduce_fusion
  227.3 62.1 %while.105 = (s32[]{:T(128)}, bf16[3,4,448,64]{2,3,1,0:T(8,128)(2,1)}, bf16[3,4,1500,64]{2,3,1,0:T(8,128)(2,1)}, bf16[3,4,1500,64]{2,3,1,0:T(8,128)(2,1)}, bf16[...) while((s32[]{:T(128)}, ...), condition=%wide.region_18.19_spmd.clone, body=%wide.region_16.18_spmd.clone.sunk | while | flops 1753456896 | bytes 91447864 | solution.py:109
  230.4 4.4 multiply_reduce_fusion.10
  237.8 3.5 fusion.276
  244.2 3.8 fusion.278
  251.1 4.4 multiply_reduce_fusion.10
  264.9 3.8 fusion.278
  271.8 4.4 multiply_reduce_fusion.10
  279.2 3.5 fusion.276
  285.6 3.8 fusion.278
  305.9 33.2 %while.106 = (s32[]{:T(128)}, bf16[3,4,448,64]{2,3,1,0:T(8,128)(2,1)}, bf16[3,4,448,64]{2,3,1,0:T(8,128)(2,1)}, bf16[3,4,448,64]{2,3,1,0:T(8,128)(2,1)}, bf16[3,...) while((s32[]{:T(128)}, ...), condition=%wide.region_23.24_spmd.clone, body=%wide.region_21.23_spmd.clone.sunk | while | flops 524179712 | bytes 31523412 | solution.py:109
  340.4 3.8 bitcast_dynamic-update-slice_fusion.9
  363.6 4.9 convolution_bitcast_fusion
  371.5 7.9 pad_maximum_fusion
  379.4 4.6 fusion.170
  387.4 25.8 %copy.88 = f32[1,1500,768]{2,0,1:T(1,128)} copy(f32[1,1500,768]{2,1,0:T(8,128)S(1)} %add_bitcast_fusion) | data formatting | bytes 9216000
  427.8 42.2 %all-reduce = f32[17,768]{1,0:T(8,128)S(1)} all-reduce(f32[17,768]{1,0:T(8,128)S(1)} %concatenate.4), channel_id=4, replica_groups=mesh['dp'=4,'fsdp'=8] {'dp','fsdp'}, use_global_device_ids=true, to_apply=%region_42.43.clone | all-reduce | flops 13056 | bytes 104448
  474.2 5.7 fusion.167
  479.9 88.4 %reduce-scatter.4.cloned.1.call-done = f32[8,24,768]{2,1,0:T(8,128)} async-done(((f32[8,768,768]{2,1,0:T(8,128)}), f32[8,24,768]{2,1,0:T(8,128)}) %reduce-scatter.4.cloned.1.call-update) | async-done | bytes 589840 | tf_op jit(solution)/shard_map/reduce_scatter | solution.py:332
  571.3 207.2 %reduce-scatter.6.cloned.1.call-done = f32[2,96,768]{2,1,0:T(8,128)} async-done(((f32[2,3072,768]{2,1,0:T(8,128)}), f32[2,96,768]{2,1,0:T(8,128)}) %reduce-scatter.6.cloned.1.call-update) | async-done | bytes 589840 | tf_op jit(solution)/shard_map/reduce_scatter | solution.py:333
  (349 shorter events, 214.0 us)
Async XLA Ops:
  7.2 130.3 %copy-start = (bf16[1,1500,768]{2,1,0:T(8,128)(2,1)S(1)}, bf16[1,1500,768]{2,1,0:T(8,128)(2,1)}, u32[]{:S(2)}) copy-start(bf16[1,1500,768]{2,1,0:T(8,128)(2,1)} %param.23) | copy-start | bytes 6912004
  7.2 89.5 %all-gather.3.cloned.1.call-start = ((), (), s32[]{:S(2)}) async-start(), calls=%async_computation.2 | async-start | bytes 9732096 | tf_op jit(solution)/shard_map/all_gather | solution.py:302
  9.2 179.7 %all-gather.5.cloned.1.call-start = ((), (), s32[]{:S(2)}) async-start(), calls=%async_computation.3 | async-start | bytes 9732096 | tf_op jit(solution)/shard_map/all_gather | solution.py:303
  11.1 557.2 %reduce-scatter.4.cloned.1.call-start = ((), (), s32[]{:S(2)}) async-start(), calls=%async_computation.4 | async-start | bytes 19464192 | tf_op jit(solution)/shard_map/reduce_scatter | solution.py:332
  59.2 47.1 %copy-start.43 = (f32[768]{0:T(1024)}, f32[768]{0:T(1024)S(1)}, u32[]{:S(2)}) copy-start(f32[768]{0:T(1024)S(1)} %get-tuple-element.527) | copy-start | bytes 9220
  59.2 47.1 %copy-start.79 = (f32[768]{0:T(1024)}, f32[768]{0:T(1024)S(1)}, u32[]{:S(2)}) copy-start(f32[768]{0:T(1024)S(1)} %get-tuple-element.526) | copy-start | bytes 9220
  59.2 74.0 %copy-start.61 = (f32[768]{0:T(1024)}, f32[768]{0:T(1024)S(1)}, u32[]{:S(2)}) copy-start(f32[768]{0:T(1024)S(1)} %get-tuple-element.522) | copy-start | bytes 9220
  59.2 74.0 %copy-start.77 = (f32[768]{0:T(1024)}, f32[768]{0:T(1024)S(1)}, u32[]{:S(2)}) copy-start(f32[768]{0:T(1024)S(1)} %get-tuple-element.521) | copy-start | bytes 9220
  59.4 46.9 %copy-start.45 = (f32[448]{0:T(512)}, f32[448]{0:T(512)S(1)}, u32[]{:S(2)}) copy-start(f32[448]{0:T(512)S(1)} %broadcast_multiply_fusion.4) | copy-start | bytes 5380
  59.7 46.5 %copy-start.56 = (f32[448]{0:T(512)}, f32[448]{0:T(512)S(1)}, u32[]{:S(2)}) copy-start(f32[448]{0:T(512)S(1)} %fusion.179) | copy-start | bytes 5380
  156.4 28.2 %copy-start.63 = (f32[768]{0:T(1024)S(1)}, f32[768]{0:T(1024)}, u32[]{:S(2)}) copy-start(f32[768]{0:T(1024)} %get-tuple-element.518) | copy-start | bytes 9220
  187.5 30.3 %copy-start.50 = (f32[448]{0:T(512)}, f32[448]{0:T(512)S(1)}, u32[]{:S(2)}) copy-start(f32[448]{0:T(512)S(1)} %broadcast_multiply_fusion.2) | copy-start | bytes 5380
  188.9 28.9 %copy-start.70 = (f32[448]{0:T(512)}, f32[448]{0:T(512)S(1)}, u32[]{:S(2)}) copy-start(f32[448]{0:T(512)S(1)} %fusion.181) | copy-start | bytes 5380
  188.9 18.0 %copy-start.30 = (bf16[1,448,768]{2,1,0:T(8,128)(2,1)S(1)}, bf16[1,448,768]{2,1,0:T(8,128)(2,1)}, u32[]{:S(2)}) copy-start(bf16[1,448,768]{2,1,0:T(8,128)(2,1)} %param.24) | copy-start | bytes 2064388
  188.9 18.0 %copy-start.47 = (f32[448]{0:T(512)S(1)}, f32[448]{0:T(512)}, u32[]{:S(2)}) copy-start(f32[448]{0:T(512)} %fusion.184) | copy-start | bytes 5380
  188.9 18.0 %copy-start.81 = (bf16[2,3072,768]{2,1,0:T(8,128)(2,1)S(1)}, bf16[2,3072,768]{2,1,0:T(8,128)(2,1)}, u32[]{:S(2)}) copy-start(bf16[2,3072,768]{2,1,0:T(8,128)(2,1)} %all-gather.5.cloned.1.call-done) | copy-start | bytes 28311556
  206.9 7.7 copy-start.6
  227.3 64.2 %copy-start.49 = (f32[448]{0:T(512)S(1)}, f32[448]{0:T(512)}, u32[]{:S(2)}) copy-start(f32[448]{0:T(512)} %copy-done.48) | copy-start | bytes 5380
  227.3 64.2 %copy-start.62 = (f32[768]{0:T(1024)S(1)}, f32[768]{0:T(1024)}, u32[]{:S(2)}) copy-start(f32[768]{0:T(1024)} %copy-done.61) | copy-start | bytes 9220
  227.3 64.2 %copy-start.69 = (f32[448]{0:T(512)S(1)}, f32[448]{0:T(512)}, u32[]{:S(2)}) copy-start(f32[448]{0:T(512)} %copy-done.68) | copy-start | bytes 5380
  305.9 34.5 %copy-start.44 = (f32[768]{0:T(1024)S(1)}, f32[768]{0:T(1024)}, u32[]{:S(2)}) copy-start(f32[768]{0:T(1024)} %copy-done.43) | copy-start | bytes 9220
  305.9 34.5 %copy-start.46 = (f32[448]{0:T(512)S(1)}, f32[448]{0:T(512)}, u32[]{:S(2)}) copy-start(f32[448]{0:T(512)} %copy-done.45) | copy-start | bytes 5380
  305.9 34.5 %copy-start.57 = (f32[448]{0:T(512)S(1)}, f32[448]{0:T(512)}, u32[]{:S(2)}) copy-start(f32[448]{0:T(512)} %copy-done.56) | copy-start | bytes 5380
  305.9 34.5 %copy-start.80 = (f32[768]{0:T(1024)S(1)}, f32[768]{0:T(1024)}, u32[]{:S(2)}) copy-start(f32[768]{0:T(1024)} %copy-done.79) | copy-start | bytes 9220
  363.4 415.1 %reduce-scatter.6.cloned.1.call-start = ((), (), s32[]{:S(2)}) async-start(), calls=%async_computation.5 | async-start | bytes 19464192 | tf_op jit(solution)/shard_map/reduce_scatter | solution.py:333
  387.4 25.8 %copy-start.19 = (bf16[3,4,448,64]{2,3,1,0:T(8,128)(2,1)S(1)}, bf16[3,4,448,64]{2,3,1,0:T(8,128)(2,1)}, u32[]{:S(2)}) copy-start(bf16[3,4,448,64]{2,3,1,0:T(8,128)(2,1)} %copy-done.18) | copy-start | bytes 2064388
  422.0 5.3 copy-start.64
  422.2 47.8 %copy-start.42 = (f32[17,24]{1,0:T(8,128)S(1)}, f32[17,24]{1,0:T(8,128)}, u32[]{:S(2)}) copy-start(f32[17,24]{1,0:T(8,128)} %param.33) | copy-start | bytes 4900
  422.2 47.8 %copy-start.66 = (f32[17,24]{1,0:T(8,128)S(1)}, f32[17,24]{1,0:T(8,128)}, u32[]{:S(2)}) copy-start(f32[17,24]{1,0:T(8,128)} %param.34) | copy-start | bytes 4900
  422.3 47.8 %copy-start.67 = (f32[17,24]{1,0:T(8,128)S(1)}, f32[17,24]{1,0:T(8,128)}, u32[]{:S(2)}) copy-start(f32[17,24]{1,0:T(8,128)} %param.35) | copy-start | bytes 4900
  474.2 94.2 %copy-start.36 = (f32[8,24,768]{2,1,0:T(8,128)S(1)}, f32[8,24,768]{2,1,0:T(8,128)}, u32[]{:S(2)}) copy-start(f32[8,24,768]{2,1,0:T(8,128)} %param.27) | copy-start | bytes 1769476
  479.9 298.6 %copy-start.37 = (f32[2,96,768]{2,1,0:T(8,128)S(1)}, f32[2,96,768]{2,1,0:T(8,128)}, u32[]{:S(2)}) copy-start(f32[2,96,768]{2,1,0:T(8,128)} %param.30) | copy-start | bytes 1769476
  (64 other events, 197.0 us)
Sparse Core Ops, SparseCore 0:
  11.6 85.0 all-gather.2
  100.2 80.6 all-gather.4
  363.5 204.8 reduce-scatter.3
  574.6 203.8 reduce-scatter.5
where the time goes:
time: 796 us; the launch traced here: 788 us
  waiting for transfers between devices  329 us (41%)
  matrix products  231 us (29%)
  blocking collectives  86.5 us (11%)
  local copies, waits for them, and re-layouts  68.5 us (9%)
  other arithmetic  54.9 us (7%)
  between operations  16.3 us (2%)
    reduce_scatter x1, waiting for transfers between devices, body(): lax.psum_scatter(totals[1], ('dp', 'fsdp'), scatter_dimension=1, tiled=True)  207 us
    reduce_scatter x1, waiting for transfers between devices, body(): lax.psum_scatter(totals[0], ('dp', 'fsdp'), scatter_dimension=1, tiled=True)  88.4 us
    dot_general x10, matrix products, outer_last(): lax.dot_general(left, right, (((1,), (1,)), ((), ())), preferred_element_...  49.3 us
    all_gather x1, blocking collectives, body(): lax.all_gather(shards[2], ('dp', 'fsdp'), axis=1, tiled=True)  44.3 us
    unnamed x1, blocking collectives  42.2 us
    dot_general x10, matrix products, matmul(): return jnp.dot(left, right, preferred_element_type=jnp.float32)  35.8 us
    unnamed x168, local copies, waits for them, and re-layouts  33.8 us
    all_gather x1, waiting for transfers between devices, body(): lax.all_gather(shards[0], ('dp', 'fsdp'), axis=1, tiled=True)  33.3 us
  transfers between devices with their start and end apart: 4, of which 3 were waited for; matrix products, arithmetic and copies ran while one was open for 22% of the time, Pallas kernels for 0%

commit v1 on v0

--- a/solution.py
+++ b/solution.py
@@ -1,6 +1,9 @@
+import functools
 import jax
 import jax.numpy as jnp
 from jax import lax
+from jax.experimental import pallas as pl
+from jax.experimental.pallas import tpu as pltpu
 from jax.sharding import PartitionSpec as P
 
 D = 768
@@ -10,9 +13,474 @@
 FRAMES = 1500
 TOK = 448
 STEP = 10
-
-
+PADDED = 1536
+ROWS = 24
+PLANE = 4
+DEPTH = 4
+UNITS = 16
+HALF = D // 2
+BF = jnp.bfloat16
+F32 = jnp.float32
+MESH = pl.DeviceIdType.MESH
 norm_epsilon = 1e-05
+MIB = 2**20
+
+
+def dot(a, b):
+    return lax.dot_general(a, b, (((1,), (0,)), ((), ())), preferred_element_type=F32)
+
+
+def dot_nt(a, b):
+    return lax.dot_general(a, b, (((1,), (1,)), ((), ())), preferred_element_type=F32)
+
+
+def dot_tn(a, b):
+    return lax.dot_general(a, b, (((0,), (0,)), ((), ())), preferred_element_type=F32)
+
+
+def layer_norm(v, gain, shift):
+    c = v - jnp.mean(v, -1, keepdims=True)
+    s = jnp.mean(c * c, -1, keepdims=True)
+    return c * lax.rsqrt(s + norm_epsilon) * gain + shift
+
+
+def layer_norm_back(v, gain, grad):
+    c = v - jnp.mean(v, -1, keepdims=True)
+    r = lax.rsqrt(jnp.mean(c * c, -1, keepdims=True) + norm_epsilon)
+    xh = c * r
+    t = grad * gain
+    dx = r * (t - jnp.mean(t, -1, keepdims=True) - xh * jnp.mean(t * xh, -1, keepdims=True))
+    return dx, jnp.sum(grad * xh, 0, keepdims=True), jnp.sum(grad, 0, keepdims=True)
+
+
+def gelu_both(u):
+    z = jnp.abs(u) * 0.7071067811865476
+    e = jnp.exp(-0.5 * u * u)
+    t = 1.0 / (1.0 + 0.3275911 * z)
+    poly = t * (0.254829592 + t * (-0.284496736 + t * (1.421413741 + t * (-1.453152027 + t * 1.061405429))))
+    half = 0.5 * poly * e
+    phi = jnp.where(u >= 0, 1.0 - half, half)
+    return u * phi, phi + u * (e * 0.3989422804014327)
+
+
+def colsum(v):
+    return jnp.sum(v.astype(F32), 0, keepdims=True)
+
+
+def head_lanes(rows, h):
+    return (lax.broadcasted_iota(jnp.int32, (rows, 128), 1) // HD) == h
+
+
+class Place:
+    def __init__(self):
+        self.z = lax.axis_index("dp")
+        f = lax.axis_index("fsdp")
+        self.f = f
+        self.c = f % 2
+        self.p = f // 2
+        x, y = self.p % 2, self.p // 2
+        self.part = f + 1 - 2 * self.c
+        fx, fy = f + 2 - 4 * x, f + 4 - 8 * y
+        px, py = self.p + 1 - 2 * x, self.p + 2 - 4 * y
+        c = self.c
+        self.n1, self.n2 = fx + c * (fy - fx), fy + c * (fx - fy)
+        self.p1, self.p2, self.p3 = px + c * (py - px), py + c * (px - py), 3 - self.p
+        self.zto = [(self.z + d) % DEPTH for d in range(1, DEPTH)]
+        self.zfrom = [(self.z + DEPTH - d) % DEPTH for d in range(1, DEPTH)]
+        self.own = pl.ds(pl.multiple_of(c * HALF, 128), HALF)
+        self.other = pl.ds(pl.multiple_of(HALF - c * HALF, 128), HALF)
+
+    def greet(self):
+        barrier = pltpu.get_barrier_semaphore()
+        others = [(zz, self.f) for zz in self.zto]
+        others += [(self.z, self.n1), (self.z, self.n2), (self.z, self.part)]
+        for device in others:
+            pl.semaphore_signal(barrier, inc=1, device_id=device, device_id_type=MESH)
+        pl.semaphore_wait(barrier, len(others))
+
+
+def remote(src, dst, send, recv, device):
+    return pltpu.make_async_remote_copy(
+        src_ref=src, dst_ref=dst, send_sem=send, recv_sem=recv, device_id=device, device_id_type=MESH
+    )
+
+
+class Gather:
+    def __init__(self, place, view, send, recv):
+        self.w, self.view, self.send, self.recv = place, view, send, recv
+
+    def copy(self, k, ref, device):
+        return remote(ref, ref, self.send(k), self.recv(k), device)
+
+    def own(self, zz, p):
+        return self.view(zz, p, True)
+
+    def s1(self):
+        w = self.w
+        for i, zz in enumerate(w.zto):
+            self.copy(i, self.own(w.z, w.p), (zz, w.f)).start()
+
+    def s2(self):
+        w = self.w
+        for i, zz in enumerate(w.zfrom):
+            self.copy(i, self.own(zz, w.p), (zz, w.f)).wait_recv()
+        self.copy(3, self.own(None, w.p), (w.z, w.n1)).start()
+        self.copy(4, self.own(None, w.p), (w.z, w.n2)).start()
+        self.copy(6, self.own(None, w.p), (w.z, w.part)).start()
+
+    def s3(self):
+        w = self.w
+        self.copy(3, self.own(None, w.p1), (w.z, w.n1)).wait_recv()
+        self.copy(5, self.own(None, w.p1), (w.z, w.n2)).start()
+        self.copy(7, self.own(None, w.p1), (w.z, w.part)).start()
+
+    def s4(self):
+        w = self.w
+        self.copy(4, self.own(None, w.p2), (w.z, w.n2)).wait_recv()
+        self.copy(8, self.own(None, w.p2), (w.z, w.part)).start()
+
+    def s5(self):
+        w = self.w
+        self.copy(5, self.own(None, w.p3), (w.z, w.n2)).wait_recv()
+        self.copy(9, self.own(None, w.p3), (w.z, w.part)).start()
+
+    def ready(self):
+        w = self.w
+        for k, p in enumerate((w.p, w.p1, w.p2, w.p3)):
+            self.copy(6 + k, self.view(None, p, False), (w.z, w.part)).wait_recv()
+
+    def drain(self):
+        w = self.w
+        for i, zz in enumerate(w.zto):
+            self.copy(i, self.own(w.z, w.p), (zz, w.f)).wait_send()
+        for k, p in ((3, w.p), (4, w.p), (5, w.p1), (6, w.p), (7, w.p1), (8, w.p2), (9, w.p3)):
+            self.copy(k, self.own(None, p), (w.z, w.n1)).wait_send()
+
+
+def heads_forward(q_ref, k_ref, v_ref, o_ref, lse_ref, mask_fn, keys, tile, first, count):
+    def pair(hp):
+        lanes = pl.ds(pl.multiple_of(hp * 128, 128), 128)
+        kp, vp = k_ref[:keys, lanes], v_ref[:keys, lanes]
+        for i in range(TOK // tile):
+            rows = pl.ds(i * tile, tile)
+            qp = q_ref[rows, lanes]
+            outs = []
+            for h in range(2):
+                s = dot_nt(jnp.where(head_lanes(tile, h), qp, jnp.zeros_like(qp)), kp)
+                s = mask_fn(s, i)
+                peak = jnp.max(s, -1, keepdims=True)
+                expo = jnp.exp(s - peak)
+                total = jnp.sum(expo, -1, keepdims=True)
+                outs.append(dot(expo.astype(BF), vp) * (1.0 / total))
+                lane = lax.broadcasted_iota(jnp.int32, (tile, 128), 1)
+                lse_ref[rows, :] = jnp.where(lane == hp * 2 + h, peak + jnp.log(total), lse_ref[rows, :])
+            o_ref[rows, lanes] = jnp.where(head_lanes(tile, 0), outs[0], outs[1]).astype(BF)
+
+    def step(i, _):
+        pair(first + i)
+        return 0
+
+    lax.fori_loop(0, count, step, 0)
+
+
+def thirds(f):
+    def step(j, _):
+        f(pl.ds(pl.multiple_of(j * 256, 256), 256))
+        return 0
+
+    lax.fori_loop(0, 3, step, 0)
+
+
+ORDER = [5, 6, 0, 1, 2, 3, 4, 7, 8, 12, 9, 13, 10, 14, 11, 15]
+A1, Q, K, V_, O, A2, CQ, O2 = range(8)
+
+
+def forward_kernel(
+    len_ref, frames_ref, x_hbm, enc_hbm, cot_hbm, attn_hbm, mlp_hbm, vec_hbm,
+    out_hbm, act_hbm, kv_hbm, lse_hbm, xs_hbm, wattn_hbm, gffn_hbm, vec_out, gv_out,
+    weights, vgather, stage, x_ref, enc, cot, act, kv, lse_cols, lse_rows, xs, hm, gp, du, oacc, dacc, grads, vec, gv,
+    load_sem, stage_sem, send_sem, recv_sem, vsend_sem, vrecv_sem, store_sem, gsem,
+    *, comm=True,
+):
+    w = Place()
+    length, frames = len_ref[0], frames_ref[0]
+    local = lambda src, dst, sem: pltpu.make_async_copy(src, dst, sem)
+    loads = [
+        local(attn_hbm.at[:, :, w.own], stage.at[pl.ds(0, 8), w.c], load_sem.at[0]),
+        local(mlp_hbm.at[:, :, w.own], stage.at[pl.ds(8, 8), w.c], load_sem.at[1]),
+        local(vec_hbm, vgather.at[w.z, w.p, w.c], load_sem.at[2]),
+        local(x_hbm, x_ref, load_sem.at[3]),
+        local(enc_hbm, enc, load_sem.at[4]),
+        local(cot_hbm, cot, load_sem.at[5]),
+    ]
+    for i in (2, 0, 1, 3, 4, 5):
+        loads[i].start()
+    w.greet()
+
+    def unit_view(u):
+        def view(zz, p, own):
+            return weights.at[u, slice(None) if zz is None else zz, p, :, w.own if own else w.other]
+        return view
+
+    def vec_view(zz, p, own):
+        return vgather.at[slice(None) if zz is None else zz, p, w.c if own else 1 - w.c]
+
+    units = [Gather(w, unit_view(u), lambda k, u=u: send_sem.at[u, k], lambda k, u=u: recv_sem.at[u, k]) for u in ORDER]
+    vecs = Gather(w, vec_view, lambda k: vsend_sem.at[k], lambda k: vrecv_sem.at[k])
+
+    loads[2].wait()
+    vecs.s1()
+    parts = ((5, 2, attn_hbm, 5), (0, 5, attn_hbm, 0), (7, 1, attn_hbm, 7), (8, 8, mlp_hbm, 0))
+    swaps = []
+    for i, (u0, n, src, at) in enumerate(parts):
+        src = src.at[pl.ds(at, n), :, w.other]
+        swaps.append(remote(src, stage.at[pl.ds(u0, n), w.c], stage_sem.at[0, i], stage_sem.at[1, i], (w.z, w.part)))
+        swaps[i].start()
+    loads[0].wait()
+    loads[1].wait()
+
+    def cast(u):
+        weights[u, w.z, w.p, :, w.own] = stage[u].reshape(2 * ROWS, HALF).astype(BF)
+
+    for i, (u0, n, _, _) in enumerate(parts):
+        swaps[i].wait_recv()
+        for u in range(u0, u0 + n):
+            cast(u)
+        if i == 0:
+            units[0].s1()
+            units[1].s1()
+            vecs.s2()
+        if i == 1:
+            units[2].s1()
+
+    def tick(t):
+        if t < UNITS:
+            units[t].s2()
+        if t + 3 < UNITS:
+            units[t + 3].s1()
+        if t >= 2 and t - 2 < UNITS:
+            units[t - 2].s5()
+        if t >= 1 and t - 1 < UNITS:
+            units[t - 1].s3()
+            units[t - 1].s4()
+
+    stores = []
+
+    def store(src, dst):
+        c = local(src, dst, store_sem.at[len(stores)])
+        c.start()
+        stores.append(c)
+
+    flat = weights
+    def wcols(u, cols):
+        return weights[u, :, :, :, cols].reshape(D, cols.size)
+
+    vrow = lambda r, cols=slice(None): vec[r : r + 1, cols]
+
+    lse_cols[...] = jnp.zeros_like(lse_cols)
+    kv[:, FRAMES // 16 * 16 :, :] = jnp.zeros((2, PADDED - FRAMES // 16 * 16, D), BF)
+    tick(0)
+    vecs.s3()
+    vecs.s4()
+    vecs.s5()
+    vecs.ready()
+    tick(1)
+    table = vgather[...].reshape(D, 128).astype(BF).astype(F32)
+    vec[...] = jnp.transpose(table)[:24, :]
+    lane = lax.broadcasted_iota(jnp.int32, (ROWS, 128), 1)
+    blocks = []
+    for chip in range(16):
+        for core in range(2):
+            acc = jnp.zeros((ROWS, 128), F32)
+            for j in range(4):
+                blk = table[(chip % 4) * 192 + core * 96 + j * ROWS :][:ROWS]
+                col = jnp.sum(jnp.where(lane == 13 + chip // 4, blk, 0.0), -1, keepdims=True)
+                acc = jnp.where(lane == j, col, acc)
+            blocks.append(acc)
+    vec[16:24, :] = jnp.transpose(jnp.concatenate(blocks, 0))[:8, :]
+    loads[3].wait()
+    act[A1] = layer_norm(x_ref[...].astype(F32), vrow(0), vrow(1)).astype(BF)
+    tick(2)
+    loads[4].wait()
+
+    def enc_project(u, which, bias):
+        for r0, r1 in ((0, 512), (512, 1024), (1024, FRAMES)):
+            e = enc[r0:r1, :]
+
+            def cols(cs):
+                r = dot(e, wcols(u, cs))
+                if bias is not None:
+                    r = r + vrow(bias, cs)
+                kv[which, r0:r1, cs] = r.astype(BF)
+
+            thirds(cols)
+
+    units[0].ready()
+    enc_project(5, 0, None)
+    tick(3)
+    units[1].ready()
+    enc_project(6, 1, 10)
+    tick(4)
+
+    def project(src, u, dst, bias, scale):
+        def cols(cs):
+            r = dot(act[src], wcols(u, cs))
+            if bias is not None:
+                r = r + vrow(bias, cs)
+            act[dst, :, cs] = (r * scale).astype(BF)
+
+        thirds(cols)
+
+    units[2].ready()
+    project(A1, 0, Q, 6, 0.125)
+    tick(5)
+    units[3].ready()
+    project(A1, 1, K, None, 1.0)
+    tick(6)
+    units[4].ready()
+    project(A1, 2, V_, 7, 1.0)
+
+    def self_mask(s, i):
+        r = lax.broadcasted_iota(jnp.int32, s.shape, 0) + i * s.shape[0]
+        c = lax.broadcasted_iota(jnp.int32, s.shape, 1)
+        return jnp.where((c <= r) & (c < length), s, -1e30)
+
+    def cross_mask(s, i):
+        c = lax.broadcasted_iota(jnp.int32, (1, PADDED - 640), 1) + 640
+        return jnp.concatenate([s[:, :640], jnp.where(c < frames, s[:, 640:], -1e30)], axis=1)
+
+    heads_forward(act.at[Q], act.at[K], act.at[V_], act.at[O], lse_cols.at[0], self_mask, TOK, 448, 0, 3)
+    tick(7)
+    heads_forward(act.at[Q], act.at[K], act.at[V_], act.at[O], lse_cols.at[0], self_mask, TOK, 448, 3, 3)
+    units[5].ready()
+
+    def residual(src, base, u, dst, bias):
+        def cols(cs):
+            xs[dst, :, cs] = base(cs) + dot(act[src], wcols(u, cs)) + vrow(bias, cs)
+
+        thirds(cols)
+
+    residual(O, lambda cs: x_ref[:, cs].astype(F32), 3, 0, 8)
+    act[A2] = layer_norm(xs[0], vrow(2), vrow(3)).astype(BF)
+    tick(8)
+    units[6].ready()
+    project(A2, 4, CQ, 9, 0.125)
+    for i in range(3):
+        heads_forward(act.at[CQ], kv.at[0], kv.at[1], act.at[O2], lse_cols.at[1], cross_mask, PADDED, 224, 2 * i, 2)
+        tick(9 + i)
+    units[7].ready()
+    residual(O2, lambda cs: xs[0, :, cs], 7, 1, 11)
+    a3 = layer_norm(xs[1], vrow(4), vrow(5)).astype(BF)
+    act[8] = a3
+    store(act.at[pl.ds(0, 8)], act_hbm)
+    store(kv, kv_hbm)
+    store(weights.at[pl.ds(0, 8)], wattn_hbm)
+    for i in range(2):
+        lse_rows[i] = jnp.transpose(lse_cols[i])[:16, :]
+    store(lse_rows, lse_hbm)
+    store(xs.at[0], xs_hbm.at[0])
+    loads[5].wait()
+    ok = lax.broadcasted_iota(jnp.int32, (TOK, 1), 0) < length
+    cot[...] = jnp.where(ok, cot[...], jnp.zeros((TOK, D), BF))
+    gv[...] = jnp.zeros_like(gv)
+    gv[12:13, :] = colsum(cot[...])
+    oacc[...] = jnp.zeros_like(oacc)
+    dacc[...] = jnp.zeros_like(dacc)
+
+    rows3 = lambda u, rs: weights.at[u].reshape(D, D)[rs, :]
+
+    gcopies = {}
+    for j in range(4):
+        units[8 + 2 * j].ready()
+        units[9 + 2 * j].ready()
+        if j >= 2:
+            gcopies[(0, j - 2)].wait()
+            gcopies[(1, j - 2)].wait()
+
+        def part(t, _):
+            rs = pl.ds(pl.multiple_of(t * 256, 256), 256)
+            u = dot_nt(act[8], rows3(8 + j, rs)) + vec[16 + j : 17 + j, rs]
+            g, d = gelu_both(u)
+            hm[:, rs] = g.astype(BF)
+            gp[:, rs] = d.astype(BF)
+            return 0
+
+        lax.fori_loop(0, 3, part, 0)
+
+        def part2(t, _):
+            rs = pl.ds(pl.multiple_of(t * 256, 256), 256)
+            oacc[:, rs] += dot(hm[...], wcols(12 + j, rs))
+            d = (dot_nt(cot[...], rows3(12 + j, rs)) * gp[:, rs].astype(F32)).astype(BF)
+            du[:, rs] = d
+            gv[13 + j : 14 + j, rs] = colsum(d)
+            return 0
+
+        lax.fori_loop(0, 3, part2, 0)
+        if j < 3:
+            tick(12 + 2 * j)
+
+        def part3(t, _):
+            rs = pl.ds(pl.multiple_of(t * 256, 256), 256)
+            grads[j % 2, 1, rs, :] = dot_tn(hm[:, rs], cot[...]).astype(BF)
+            grads[j % 2, 0, rs, :] = dot_tn(du[:, rs], act[8]).astype(BF)
+            dacc[:, rs] += dot(du[...], wcols(8 + j, rs))
+            return 0
+
+        lax.fori_loop(0, 3, part3, 0)
+        for k in range(2):
+            cp = local(grads.at[j % 2, k], gffn_hbm.at[4 * k + j], gsem.at[j % 2, k])
+            cp.start()
+            gcopies[(k, j)] = cp
+        if j < 3:
+            tick(13 + 2 * j)
+    act[8] = (xs[1] + oacc[...] + vrow(12)).astype(BF)
+    store(act.at[8], out_hbm)
+    dx, gg, gb = layer_norm_back(xs[1], vrow(4), dacc[...])
+    gv[4:5, :] = gg
+    gv[5:6, :] = gb
+    oacc[...] = cot[...].astype(F32) + dx
+    store(oacc, xs_hbm.at[1])
+    store(vec, vec_out)
+    store(gv, gv_out)
+    for j in (2, 3):
+        gcopies[(0, j)].wait()
+        gcopies[(1, j)].wait()
+    for s in swaps:
+        s.wait_send()
+    vecs.drain()
+    for u in units:
+        u.drain()
+    for c in stores:
+        c.wait()
+
+
+def call_forward(length, frames, x, enc, cot, attn_w, mlp_w, vec_t):
+    any_ = pl.BlockSpec(memory_space=pl.ANY)
+    smem = pl.BlockSpec(memory_space=pltpu.SMEM)
+    t = lambda *s, dt=BF: jax.ShapeDtypeStruct(s, dt)
+    v = pltpu.VMEM
+    dma = pltpu.SemaphoreType.DMA
+    return pl.pallas_call(
+        forward_kernel,
+        out_shape=[
+            t(TOK, D), t(8, TOK, D), t(2, PADDED, D), t(2, 16, TOK, dt=F32), t(2, TOK, D, dt=F32),
+            t(8, DEPTH, PLANE, 2 * ROWS, D), t(8, D, D), t(24, D, dt=F32), t(24, D, dt=F32),
+        ],
+        in_specs=[smem, smem] + [any_] * 6,
+        out_specs=[any_] * 9,
+        scratch_shapes=[
+            v((UNITS, DEPTH, PLANE, 2 * ROWS, D), BF), v((DEPTH, PLANE, 2, ROWS, 128), F32), v((UNITS, 2, ROWS, HALF), F32),
+            v((TOK, D), BF), v((FRAMES, D), BF), v((TOK, D), BF), v((9, TOK, D), BF), v((2, PADDED, D), BF),
+            v((2, TOK, 128), F32), v((2, 16, TOK), F32), v((2, TOK, D), F32),
+            v((TOK, D), BF), v((TOK, D), BF), v((TOK, D), BF), v((TOK, D), F32), v((TOK, D), F32),
+            v((2, 2, D, D), BF), v((24, D), F32), v((24, D), F32),
+            dma((6,)), dma((2, 4)), dma((UNITS, 10)), dma((UNITS, 10)), dma((10,)), dma((10,)), dma((12,)), dma((2, 2)),
+        ],
+        compiler_params=pltpu.CompilerParams(collective_id=0, has_side_effects=True, vmem_limit_bytes=63 * MIB),
+        name="forward",
+    )(length, frames, x, enc, cot, attn_w, mlp_w, vec_t)
+
+
 beta_first = 0.9
 beta_second = 0.999
 adam_epsilon = 1e-08
@@ -281,7 +749,7 @@
     return (weight - rate * (ratio + weight_decay * weight), first_new, second_new)
 
 
-def body(
+def plain_body(
     tokens,
     enc_states,
     cotangent,
@@ -352,9 +820,61 @@
     )
 
 
+def attention_backward(x, enc, length, frames, weights, act, kv, lse, xs, vec, gv):
+    scale = HD ** (-0.5)
+    place, causal, seen = make_masks(length, frames)
+    sums = lse[:, :H].reshape(2, H // head_group(), head_group(), TOK)
+    first, query, keys, values, mixed, second, cross_query, heard = [act[i] for i in range(8)]
+    dx = xs[1]
+    out_two = dx.astype(BF)
+    g_co = inner_rows(heard, out_two)
+    b_co = colsum(out_two)[0]
+    gh = outer_last(out_two, weights[7]).astype(BF)
+    gcq, gck, gcv = attend_backward(cross_query, kv[0, :FRAMES], kv[1, :FRAMES], sums[1], gh, seen)
+    gcq = gcq * scale
+    g_enc = outer_last(gck, weights[5]) + outer_last(gcv, weights[6])
+    _, pull = jax.vjp(norm_apply, xs[0], vec[2], vec[3])
+    part, g2, b2 = pull(outer_last(gcq, weights[4]))
+    dx = dx + part
+    out_one = dx.astype(BF)
+    gm = outer_last(out_one, weights[3]).astype(BF)
+    gq, gk, gvv = attend_backward(query, keys, values, sums[0], gm, causal)
+    gq = gq * scale
+    _, pull = jax.vjp(norm_apply, x.astype(F32), vec[0], vec[1])
+    part, g1, b1 = pull(outer_last(gq, weights[0]) + outer_last(gk, weights[1]) + outer_last(gvv, weights[2]))
+    g_attn = [
+        inner_rows(first, gq), inner_rows(first, gk), inner_rows(first, gvv), inner_rows(mixed, out_one),
+        inner_rows(second, gcq), inner_rows(enc, gck), inner_rows(enc, gcv), g_co,
+    ]
+    up = gv[13:17].reshape(4, 16, 2, ROWS).transpose(1, 2, 0, 3).reshape(4, D)
+    rows = [g1, b1, g2, b2, gv[4], gv[5], colsum(gq)[0], colsum(gvv)[0], colsum(out_one)[0], colsum(gcq)[0],
+            colsum(gcv)[0], b_co, gv[12]]
+    return jnp.stack(g_attn), jnp.concatenate([jnp.stack(rows), up], 0), dx + part, g_enc
+
+
+def fused_body(tokens, enc_states, cotangent, tok_len, frame_count, attn_w, attn_m, attn_v, mlp_w, mlp_m, mlp_v, vec_w, vec_m, vec_v):
+    vec_t = jnp.pad(vec_w.T, ((0, 0), (0, 128 - vec_w.shape[0])))
+    out, act, kv, lse, xs, wattn, gffn, vec, gv = call_forward(
+        tok_len, frame_count, tokens[0], enc_states[0], cotangent[0], attn_w, mlp_w.reshape(8, ROWS, D), vec_t
+    )
+    g_attn, g_vec, d_tokens, d_enc = attention_backward(
+        tokens[0], enc_states[0], tok_len[0], frame_count[0], wattn.reshape(8, D, D), act, kv, lse, xs, vec, gv
+    )
+    g_mlp = gffn.reshape(2, 4, 16, 2, ROWS, D).transpose(0, 2, 3, 1, 4, 5).reshape(2, FF, D)
+    scatter = lambda g: lax.psum_scatter(g, ("dp", "fsdp"), scatter_dimension=1, tiled=True)
+    grad_attn = scatter(g_attn.astype(BF)).astype(F32)
+    grad_mlp = scatter(g_mlp).astype(F32)
+    grad_vec = scatter(g_vec)
+    attn_new = adam_update(attn_w, attn_m, attn_v, grad_attn, rate_attention)
+    mlp_new = adam_update(mlp_w, mlp_m, mlp_v, grad_mlp, rate_feedforward)
+    vec_new = adam_update(vec_w, vec_m, vec_v, grad_vec, rate_vector)
+    return (out[None], d_tokens[None], d_enc[None], *attn_new, *mlp_new, *vec_new)
+
+
 def solution(mesh):
+    fused = mesh.shape["dp"] == DEPTH and mesh.shape["fsdp"] == 2 * PLANE
     return jax.shard_map(
-        body,
+        fused_body if fused else plain_body,
         mesh=mesh,
         in_specs=(
             P(("dp", "fsdp"), None, None),

time: 796 us -> 613 us (0.77)
  waiting for transfers between devices: 329 us -> 171 us
  Pallas kernels: 0 us -> 128 us
  matrix products: 231 us -> 116 us
  blocking collectives: 86.5 us -> 43.2 us
  local copies, waits for them, and re-layouts: 68.5 us -> 89.3 us
  other arithmetic: 54.9 us -> 37.8 us
    reduce_scatter x2 -> x1, waiting for transfers between devices: 296 us -> 138 us  [fused_body(): lax.psum_scatter(g, ('dp', 'fsdp'), scatter_dimension=1, tiled=True)]
    pallas_call x0 -> x1, Pallas kernels: none -> 128 us  [call_forward(): pl.pallas_call(forward_kernel, out_shape=[t(TOK, D), t(8, TOK, D), t(2, P...]
    dot_general x16 -> x0, matrix products: 57.4 us -> none  [the longest x10 35.8 us: matmul(): return jnp.dot(left, right, preferred_element_type=jnp.float32)]
    all_gather x1 -> x0, blocking collectives: 44.3 us -> none  [body(): lax.all_gather(shards[2], ('dp', 'fsdp'), axis=1, tiled=True)]
    all_gather x2 -> x0, waiting for transfers between devices: 33.3 us -> none  [the longest x1 33.3 us: body(): lax.all_gather(shards[0], ('dp', 'fsdp'), axis=1, tiled=True)]
    unnamed x4 -> x3, waiting for transfers between devices: 0.07 us -> 33.3 us
    dot_general x10 -> x8, matrix products: 49.3 us -> 16.3 us  [outer_last(): lax.dot_general(left, right, (((1,), (1,)), ((), ())), preferred_element_...]
    slice x3 -> x14, local copies, waits for them, and re-layouts: 4.73 us -> 28 us  [the longest x2 8.32 us: attention_backward(): kv[1, :FRAMES]]
  transfers between devices with their start and end apart: 4 -> 2, of which waited for: 3 -> 2; matrix products, arithmetic and copies ran while one was open for 22% -> 10% of each run, Pallas kernels for 0% -> 0%
where the time goes in v1:
time: 613 us; the launch traced here: 602 us
  waiting for transfers between devices  171 us (28%)
  Pallas kernels  128 us (21%)
  matrix products  116 us (19%)
  local copies, waits for them, and re-layouts  89.3 us (15%)
  blocking collectives  43.2 us (7%)
  other arithmetic  37.8 us (6%)
  between operations  16.1 us (3%)
    reduce_scatter x1, waiting for transfers between devices, fused_body(): lax.psum_scatter(g, ('dp', 'fsdp'), scatter_dimension=1, tiled=True)  138 us
    pallas_call x1, Pallas kernels, call_forward(): pl.pallas_call(forward_kernel, out_shape=[t(TOK, D), t(8, TOK, D), t(2, P...  128 us
    unnamed x1, blocking collectives  43.2 us
    unnamed x79, local copies, waits for them, and re-layouts  39.8 us
    unnamed x3, waiting for transfers between devices  33.3 us
    dot_general x8, matrix products, inner_rows(): lax.dot_general(left, right, (((0,), (0,)), ((), ())), preferred_element_...  20.1 us
    dot_general x6, matrix products, one_group(): jnp.einsum('gtd,gsd->gts', g_group, v_group, preferred_element_type=jnp.f...  19.9 us
    dot_general x6, matrix products, one_group(): jnp.einsum('gts,gsd->gtd', grad_scores, k_group, preferred_element_type=j...  16.8 us
  transfers between devices with their start and end apart: 2, of which 2 were waited for; matrix products, arithmetic and copies ran while one was open for 10% of the time, Pallas kernels for 0%

profile of v1, /device:TPU:0, one launch (start us, length us, event | category | flops | bytes accessed | tf_op | source)
XLA Modules:
  0.0 602.4 jit_solution(3239650329031756552)
XLA Ops:
  12.3 128.1 %forward.1 = (bf16[448,768]{1,0:T(8,128)(2,1)}, bf16[8,448,768]{2,1,0:T(8,128)(2,1)}, bf16[2,1536,768]{2,1,0:T(8,128)(2,1)}, f32[2,16,448]{2,1,0:T(8,128)}, f32[...) custom-call(s32[1]{0:T(128)} %copy.132.len_ref, ...), custom_call_target="tpu_custom_call" | custom-call | tf_op jit(solution)/shard_map/forward/pallas_call | solution.py:463
  152.2 4.1 fusion.147
  156.3 4.3 copy.67
  163.0 6.9 %fusion.145 = (bf16[1,4,4,48,768]{4,3,2,1,0:T(8,128)(2,1)}, bf16[1,4,4,48,768]{4,3,2,1,0:T(8,128)(2,1)}, bf16[1,4,4,48,768]{4,3,2,1,0:T(8,128)(2,1)}, bf16[1,4,4...) fusion(bf16[8,4,4,48,768]{4,3,2,1,0:T(8,128)(2,1)} %get-tuple-e, ...), kind=kLoop, calls=%fused_computation.189 | loop fusion | bytes 18874368 | tf_op jit(solution)/shard_map/slice | solution.py:835
  174.7 58.7 %while.30 = (s32[]{:T(128)}, bf16[3,4,448,64]{2,3,1,0:T(8,128)(2,1)}, bf16[3,4,1500,64]{2,3,1,0:T(8,128)(2,1)}, bf16[3,4,1500,64]{2,3,1,0:T(8,128)(2,1)}, bf16[3...) while((s32[]{:T(128)}, ...), condition=%wide.region_2.3_spmd.clone, body=%wide.region_0.0_spmd.clone.sunk | while | flops 1753456896 | bytes 89214576 | solution.py:577
  174.9 2.9 fusion.210
  180.8 4.3 multiply_reduce_fusion.7
  185.1 2.9 multiply_convert_fusion.4
  188.0 3.5 fusion.211
  191.5 2.9 fusion.212
  194.4 2.9 fusion.210
  200.2 4.3 multiply_reduce_fusion.7
  204.6 2.9 multiply_convert_fusion.4
  207.5 3.5 fusion.211
  211.0 2.9 fusion.212
  213.9 2.9 fusion.210
  219.7 4.3 multiply_reduce_fusion.7
  224.1 2.9 multiply_convert_fusion.4
  227.0 3.5 fusion.211
  234.7 2.9 multiply_reduce_fusion.2
  247.2 36.0 %while.31 = (s32[]{:T(128)}, bf16[3,4,448,64]{2,3,1,0:T(8,128)(2,1)}, bf16[3,4,448,64]{2,3,1,0:T(8,128)(2,1)}, bf16[3,4,448,64]{2,3,1,0:T(8,128)(2,1)}, bf16[3,4...) while((s32[]{:T(128)}, ...), condition=%wide.region_9.10_spmd.clone, body=%wide.region_7.9_spmd.clone.sunk | while | flops 524179712 | bytes 31294036 | solution.py:577
  284.5 3.3 fusion.96
  287.8 3.1 fusion.98
  296.6 3.2 fusion.92
  299.8 3.1 fusion.94
  304.7 8.7 %copy.86 = bf16[96,8,8,768]{3,1,2,0:T(8,128)(2,1)} copy(bf16[96,8,8,768]{3,1,0,2:T(8,128)(2,1)} %bitcast.255) | data formatting | bytes 18874368
  313.9 8.7 %copy.74 = bf16[2,16,2,4,24,768]{5,4,3,2,1,0:T(8,128)(2,1)} copy(bf16[2,16,2,4,24,768]{5,4,2,1,3,0:T(8,128)(2,1)} %bitcast.355) | data formatting | bytes 18874368 | tf_op jit(solution)/shard_map/transpose | solution.py:863
  343.4 26.0 %copy.76 = f32[1,1500,768]{2,0,1:T(1,128)} copy(f32[1,1500,768]{2,1,0:T(8,128)S(1)} %add_bitcast_fusion) | data formatting | bytes 9216000
  369.5 43.2 %all-reduce.1 = f32[17,768]{1,0:T(8,128)S(1)} all-reduce(f32[17,768]{1,0:T(8,128)S(1)} %concatenate.4), channel_id=4, replica_groups=mesh['dp'=4,'fsdp'=8] {'dp','fsdp'}, use_global_device_ids=true, to_apply=%region_26.27.clone | all-reduce | flops 13056 | bytes 104448
  413.5 3.7 add_bitcast_fusion.1
  417.2 33.2 %reduce-scatter.8.cloned.1.call-done = bf16[24,6144]{1,0:T(8,128)(2,1)} async-done(((bf16[768,6144]{1,0:T(8,128)(2,1)}), bf16[24,6144]{1,0:T(8,128)(2,1)}) %reduce-scatter.8.cloned.1.call-update) | async-done | bytes 294928
  454.2 137.8 %reduce-scatter.6.cloned.1.call-done = bf16[2,96,768]{2,1,0:T(8,128)(2,1)} async-done(((bf16[2,3072,768]{2,1,0:T(8,128)(2,1)}), bf16[2,96,768]{2,1,0:T(8,128)(2,1)}) %reduce-scatter.6.cloned.1.call-update) | async-done | bytes 294928 | tf_op jit(solution)/shard_map/reduce_scatter | solution.py:864
  (194 shorter events, 118.8 us)
Async XLA Ops:
  7.2 443.3 %reduce-scatter.8.cloned.1.call-start = ((), (), s32[]{:S(2)}) async-start(), calls=%async_computation.3 | async-start | bytes 9732096
  140.4 4.6 copy-start.28
  163.0 6.9 %copy-start = (f32[2,448,768]{2,1,0:T(8,128)S(1)}, f32[2,448,768]{2,1,0:T(8,128)}, u32[]{:S(2)}) copy-start(f32[2,448,768]{2,1,0:T(8,128)} %get-tuple-element.130) | copy-start | bytes 8257540
  174.9 2.9 copy-start.4
  194.4 2.9 copy-start.4
  213.9 2.9 copy-start.4
  234.6 2.9 copy-start.8
  234.7 3.0 copy-start.32
  242.0 5.2 copy-start.33
  247.4 2.6 copy-start.5
  259.4 2.6 copy-start.5
  271.3 2.6 copy-start.5
  284.5 6.5 %copy-start.3 = (bf16[3,4,448,64]{2,3,1,0:T(8,128)(2,1)}, bf16[3,4,448,64]{2,3,1,0:T(8,128)(2,1)S(1)}, u32[]{:S(2)}) copy-start(bf16[3,4,448,64]{2,3,1,0:T(8,128)(2,1)S(1)} %broadcast_multiply_fusion) | copy-start | bytes 2064388
  284.5 3.4 copy-start.12
  284.5 6.4 %copy-start.18 = (bf16[8,448,768]{2,1,0:T(8,128)(2,1)S(1)}, bf16[8,448,768]{2,1,0:T(8,128)(2,1)}, u32[]{:S(2)}) copy-start(bf16[8,448,768]{2,1,0:T(8,128)(2,1)} %get-tuple-element.131) | copy-start | bytes 16515076
  287.8 3.1 copy-start.10
  292.8 3.7 copy-start.37
  296.6 3.2 copy-start.13
  313.4 278.6 %reduce-scatter.6.cloned.1.call-start = ((), (), s32[]{:S(2)}) async-start(), calls=%async_computation.2 | async-start | bytes 9732096 | tf_op jit(solution)/shard_map/reduce_scatter | solution.py:864
  331.8 2.6 copy-start.7
  334.4 2.3 copy-start.2
  334.4 2.3 copy-start.11
  336.7 2.4 copy-start.20
  336.7 2.4 copy-start.38
  343.3 69.4 %copy-start.29 = (f32[17,24]{1,0:T(8,128)S(1)}, f32[17,24]{1,0:T(8,128)}, u32[]{:S(2)}) copy-start(f32[17,24]{1,0:T(8,128)} %param.29) | copy-start | bytes 4900
  343.4 69.4 %copy-start.34 = (f32[17,24]{1,0:T(8,128)S(1)}, f32[17,24]{1,0:T(8,128)}, u32[]{:S(2)}) copy-start(f32[17,24]{1,0:T(8,128)} %param.30) | copy-start | bytes 4900
  343.4 69.4 %copy-start.35 = (f32[17,24]{1,0:T(8,128)S(1)}, f32[17,24]{1,0:T(8,128)}, u32[]{:S(2)}) copy-start(f32[17,24]{1,0:T(8,128)} %param.31) | copy-start | bytes 4900
  413.5 38.0 %copy-start.15 = (f32[8,24,768]{2,1,0:T(8,128)S(1)}, f32[8,24,768]{2,1,0:T(8,128)}, u32[]{:S(2)}) copy-start(f32[8,24,768]{2,1,0:T(8,128)} %attn_hbm.1) | copy-start | bytes 1769476
  417.2 174.8 %copy-start.16 = (f32[2,96,768]{2,1,0:T(8,128)S(1)}, f32[2,96,768]{2,1,0:T(8,128)}, u32[]{:S(2)}) copy-start(f32[2,96,768]{2,1,0:T(8,128)} %param.26) | copy-start | bytes 1769476
  417.2 174.8 %copy-start.26 = (f32[2,96,768]{2,1,0:T(8,128)S(1)}, f32[2,96,768]{2,1,0:T(8,128)}, u32[]{:S(2)}) copy-start(f32[2,96,768]{2,1,0:T(8,128)} %param.27) | copy-start | bytes 1769476
  417.2 174.8 %copy-start.27 = (f32[2,96,768]{2,1,0:T(8,128)S(1)}, f32[2,96,768]{2,1,0:T(8,128)}, u32[]{:S(2)}) copy-start(f32[2,96,768]{2,1,0:T(8,128)} %param.28) | copy-start | bytes 1769476
  454.2 140.2 %copy-start.23 = (bf16[448,768]{1,0:T(8,128)(2,1)S(1)}, bf16[448,768]{1,0:T(8,128)(2,1)}, u32[]{:S(2)}) copy-start(bf16[448,768]{1,0:T(8,128)(2,1)} %get-tuple-element.129) | copy-start | bytes 2064388
  (13 other events, 21.8 us)
Sparse Core Ops, SparseCore 0:
  313.5 136.8 reduce-scatter.7
  457.4 134.6 reduce-scatter.5
